TPU v7x, 32 devices: a whole 2x2x4 slice. The times are simulated.
32 devices in a mesh: row: 4 (over y, core), col: 8 (over z, x).
Axes of the slice: x: 2, y: 2, z: 4, core: 2. Of those that a mesh axis runs over, the one named last changes fastest.
Arguments:
- sigma_top: float32 [6144, 6144], P('row', 'col')
- factor_cross: float32 [6144, 6144], P('row', 'col'), may hold values from -0.078125 to 0.078125
- factor_inverse: float32 [6144, 6144], P('row', 'col')
- block_inverse: float32 [6144, 6144], P('row', 'col')
- ancestors: int32 [12], replicated, may hold values from 0 to 23, as said below
Outputs:
- sigma_cross: float32 [6144, 6144], P('row', 'col')
- sigma_child: float32 [6144, 6144], P('row', 'col')
Inputs may be any that keep to these rules, and one draw needn't show every extreme that they name: `ancestors`: 12 distinct block numbers; block 0 and block 23 are always among them.
All inputs are finite; a program needn't handle non-finite values.
Results may differ from a plain program's by a relative error of at most 0.000078.
Values sent between devices are 32-bit elements; how exact they have to be, the bound alone decides.
A program may use at most 192 MiB of HBM per device.

v0:
```python
import jax
import jax.numpy as jnp
from jax import lax
from jax.sharding import PartitionSpec as P

BLK = 256


def transposed_rows(gathered, right_side):
    return lax.dot_general(
        gathered,
        right_side,
        (((0,), (0,)), ((), ())),
        precision=lax.Precision.HIGHEST,
        preferred_element_type=jnp.float32,
    )


def per_device(sigma_top, factor_cross, factor_inverse, block_inverse, ancestors):
    height = sigma_top.shape[0]
    first_row = lax.axis_index("row") * height
    blocks = (first_row + lax.iota(jnp.int32, height)) // BLK
    living = jnp.any(blocks[:, None] == ancestors[None, :], axis=1)
    masked = jnp.where(living[:, None], factor_cross, jnp.float32(0.0))
    inverse_strip = lax.all_gather(factor_inverse, "row", axis=0, tiled=True)
    rows_used = inverse_strip
    update = jnp.dot(
        lax.all_gather(masked, "col", axis=1, tiled=True),
        rows_used,
        precision=lax.Precision.HIGHEST,
        preferred_element_type=jnp.float32,
    )
    update_strip = lax.all_gather(update, "row", axis=0, tiled=True)
    rows_used = update_strip
    product = jnp.dot(
        lax.all_gather(sigma_top, "col", axis=1, tiled=True),
        rows_used,
        precision=lax.Precision.HIGHEST,
        preferred_element_type=jnp.float32,
    )
    sigma_cross = jnp.where(living[:, None], -product, jnp.float32(0.0))
    gathered = lax.all_gather(sigma_cross, "col", axis=1, tiled=True)
    correction = lax.psum_scatter(
        transposed_rows(gathered, update), "row", scatter_dimension=0, tiled=True
    )
    sigma_child = block_inverse - correction
    return (sigma_cross, sigma_child)


def solution(mesh):
    return jax.shard_map(
        per_device,
        mesh=mesh,
        in_specs=(P("row", "col"), P("row", "col"), P("row", "col"), P("row", "col"), P()),
        out_specs=(P("row", "col"), P("row", "col")),
        check_vma=False,
    )
```

profile of v0, /device:TPU:0, one launch (start us, length us, event | category | flops | bytes accessed | tf_op | source)
XLA Modules:
  0.0 2861.3 jit_solution(14071378845009714266)
XLA Ops:
  7.2 0.0 copy-start
  7.2 0.0 all-gather.8.cloned.1.call-start
  7.2 0.7 all-gather.8.cloned.1.call-update
  7.9 0.0 all-gather.6.cloned.1.call-start
  8.0 0.0 copy-done
  8.0 0.1 compare_reduce_fusion
  8.1 4.9 broadcast_select_fusion
  13.0 0.0 all-gather.6.cloned.1.call-update
  13.0 0.0 all-gather.12.cloned.1.call-start
  13.1 0.7 all-gather.12.cloned.1.call-update
  13.8 0.0 all-gather.10.cloned.1.call-start
  13.8 118.5 %all-gather.8.cloned.1.call-done = f32[6144,768]{1,0:T(8,128)} async-done(((f32[1536,768]{1,0:T(8,128)}), f32[6144,768]{1,0:T(8,128)}) %all-gather.8.cloned.1.call-update) | async-done | bytes 18874384 | tf_op jit(solution)/shard_map/all_gather | solution.py:25
  132.3 718.5 %all-gather.6.cloned.1.call-done = f32[1536,6144]{1,0:T(8,128)} async-done(((f32[1536,768]{1,0:T(8,128)}), f32[1536,6144]{1,0:T(8,128)}) %all-gather.6.cloned.1.call-update) | async-done | bytes 37748752 | tf_op jit(solution)/shard_map/all_gather | solution.py:28
  850.8 99.9 %fusion.3 = f32[1536,768]{1,0:T(8,128)} fusion(f32[1536,6144]{1,0:T(8,128)} %all-gather.6.cloned.1.call-done, f32[6144,768]{1,0:T(8,128)} %all-gather.8.cloned.1.call-done), kind=kOutput, calls=%fused_computation.12 | convolution fusion | flops 86973087744 | bytes 61341696 | tf_op jit(solution)/shard_map/dot_general | solution.py:27
  950.8 0.0 all-gather.10.cloned.1.call-update
  950.8 0.0 all-gather.14.cloned.1.call-start
  950.8 617.9 %all-gather.12.cloned.1.call-done = f32[1536,6144]{1,0:T(8,128)} async-done(((f32[1536,768]{1,0:T(8,128)}), f32[1536,6144]{1,0:T(8,128)}) %all-gather.12.cloned.1.call-update) | async-done | bytes 37748752 | tf_op jit(solution)/shard_map/all_gather | solution.py:36
  1568.8 122.0 %all-gather.10.cloned.1.call-done = f32[6144,768]{1,0:T(8,128)} async-done(((f32[1536,768]{1,0:T(8,128)}), f32[6144,768]{1,0:T(8,128)}) %all-gather.10.cloned.1.call-update) | async-done | bytes 18874384 | tf_op jit(solution)/shard_map/all_gather | solution.py:33
  1690.8 182.2 %select_bitcast_fusion = f32[1536,768]{0,1:T(8,128)} fusion(f32[6144,768]{1,0:T(8,128)} %all-gather.10.cloned.1.call-done, f32[1536,6144]{1,0:T(8,128)} %all-gather.12.cloned.1.call-done, pred[1536]{0:T(1024)(128)(4,1)S(1)} %compare_reduce_fusion), kind=kOutput, calls=%fused_computation | convolution fusion | flops 86975447040 | bytes 61343232 | tf_op jit(solution)/shard_map/dot_general | solution.py:35
  1873.0 0.0 all-gather.14.cloned.1.call-update
  1873.0 0.0 reduce-scatter.2.cloned.1.call-start
  1873.0 716.5 %all-gather.14.cloned.1.call-done = f32[1536,6144]{0,1:T(8,128)} async-done(((f32[1536,768]{0,1:T(8,128)}), f32[1536,6144]{0,1:T(8,128)}) %all-gather.14.cloned.1.call-update) | async-done | bytes 37748752 | tf_op jit(solution)/shard_map/all_gather | solution.py:42
  2589.5 118.8 %fusion.4 = f32[6144,768]{1,0:T(8,128)} fusion(f32[1536,6144]{0,1:T(8,128)} %all-gather.14.cloned.1.call-done, f32[1536,768]{1,0:T(8,128)} %fusion.3), kind=kOutput, calls=%fused_computation.13 | convolution fusion | flops 86973087744 | bytes 61341696 | tf_op jit(solution)/shard_map/dot_general | solution.py:10
  2708.3 0.0 reduce-scatter.2.cloned.1.call-update
  2708.3 6.0 copy.8
  2714.4 133.5 %reduce-scatter.2.cloned.1.call-done = f32[1536,768]{1,0:T(8,128)} async-done(((f32[6144,768]{1,0:T(8,128)}), f32[1536,768]{1,0:T(8,128)}) %reduce-scatter.2.cloned.1.call-update) | async-done | bytes 4718608 | tf_op jit(solution)/shard_map/reduce_scatter | solution.py:43
  2847.9 6.6 sub.10
  (1 shorter events, 0.0 us)
Async XLA Ops:
  7.2 0.8 copy-start
  7.2 125.2 %all-gather.8.cloned.1.call-start = ((), (), s32[]{:S(2)}) async-start(), calls=%async_computation.2 | async-start | bytes 23592960 | tf_op jit(solution)/shard_map/all_gather | solution.py:25
  7.9 842.9 %all-gather.6.cloned.1.call-start = ((), (), s32[]{:S(2)}) async-start(), calls=%async_computation.1 | async-start | bytes 42467328 | tf_op jit(solution)/shard_map/all_gather | solution.py:28
  13.0 1555.7 %all-gather.12.cloned.1.call-start = ((), (), s32[]{:S(2)}) async-start(), calls=%async_computation.4 | async-start | bytes 42467328 | tf_op jit(solution)/shard_map/all_gather | solution.py:36
  13.8 1677.0 %all-gather.10.cloned.1.call-start = ((), (), s32[]{:S(2)}) async-start(), calls=%async_computation.3 | async-start | bytes 23592960 | tf_op jit(solution)/shard_map/all_gather | solution.py:33
  950.8 1638.7 %all-gather.14.cloned.1.call-start = ((), (), s32[]{:S(2)}) async-start(), calls=%async_computation.5 | async-start | bytes 42467328 | tf_op jit(solution)/shard_map/all_gather | solution.py:42
  1873.0 974.9 %reduce-scatter.2.cloned.1.call-start = ((), (), s32[]{:S(2)}) async-start(), calls=%async_computation.6 | async-start | bytes 23592960 | tf_op jit(solution)/shard_map/reduce_scatter | solution.py:43
Sparse Core Ops, SparseCore 0:
  9.6 122.7 all-gather.7
  134.4 716.3 all-gather.5
  852.4 716.3 all-gather.11
  1570.8 119.9 all-gather.9
  1873.1 716.3 all-gather.13
  2708.4 139.3 reduce-scatter.1
where the time goes:
time: 2860 us
  waiting for transfers between devices  2430 us (85%)
  matrix products  401 us (14%)
    all_gather x1, waiting for transfers between devices, per_device(): lax.all_gather(masked, 'col', axis=1, tiled=True)  719 us
    all_gather x1, waiting for transfers between devices, per_device(): gathered = lax.all_gather(sigma_cross, 'col', axis=1, tiled=True)  716 us
    all_gather x1, waiting for transfers between devices, per_device(): lax.all_gather(sigma_top, 'col', axis=1, tiled=True)  618 us
    dot_general x1, matrix products, per_device(): jnp.dot(lax.all_gather(sigma_top, 'col', axis=1, tiled=True), rows_used,...  182 us
    reduce_scatter x1, waiting for transfers between devices, per_device(): lax.psum_scatter(transposed_rows(gathered, update), 'row', scatter_dimens...  134 us
    all_gather x1, waiting for transfers between devices, per_device(): update_strip = lax.all_gather(update, 'row', axis=0, tiled=True)  122 us
    dot_general x1, matrix products, transposed_rows(): lax.dot_general(gathered, right_side, (((0,), (0,)), ((), ())), precision...  119 us
    all_gather x1, waiting for transfers between devices, per_device(): inverse_strip = lax.all_gather(factor_inverse, 'row', axis=0, tiled=True)  119 us
  transfers between devices with their start and end apart: 6, of which 6 were waited for; matrix products, arithmetic and copies ran while one was open for 4% of the time, Pallas kernels for 0%

commit v1 on v0

v1 whole, which is shorter than its diff:
```python
import functools

import jax
import jax.numpy as jnp
from jax import lax
from jax.experimental import pallas as pl
from jax.experimental.pallas import tpu as pltpu
from jax.sharding import PartitionSpec as P

BLK = 256
CHIPS_Z = 4


def gather_kernel(nz, nx, own_ref, out_ref, send_sem, recv_sem, local_sem):
    col = lax.axis_index("col")
    z, x = col // nx, col % nx
    width = own_ref.shape[1]
    up, down, right, left = 0, 1, 2, 3
    step = {up: nx, down: -nx, right: 1, left: -1}
    exists = {up: z < nz - 1, down: z > 0, right: x < nx - 1, left: x > 0}

    def place(block):
        return out_ref.at[:, pl.ds(pl.multiple_of(block * width, 128), width)]

    def copy(block, way, own=False):
        return pltpu.make_async_remote_copy(
            src_ref=own_ref if own else place(block),
            dst_ref=place(block),
            send_sem=send_sem.at[way, block],
            recv_sem=recv_sem.at[block],
            device_id={"col": col + step[way]},
            device_id_type=pl.DeviceIdType.MESH,
        )

    def walk(on_arrival, act):
        for way in (up, down, right, left):
            pl.when(exists[way])(functools.partial(act, col, way, True))
        for hop in range(1, nz):
            for way, there in ((up, z - hop >= 0), (down, z + hop < nz)):
                block = col - hop * step[way]

                @pl.when(there)
                def _(block=block, way=way):
                    on_arrival(block, way)
                    for onward in (way, right, left):
                        pl.when(exists[onward])(functools.partial(act, block, onward, False))

        for hop in range(1, nx):
            for line in range(nz):
                for way, there in ((right, x - hop >= 0), (left, x + hop < nx)):
                    block = lax.rem(z + line, nz) * nx + x - hop * step[way]

                    @pl.when(there)
                    def _(block=block, way=way):
                        on_arrival(block, way)
                        pl.when(exists[way])(functools.partial(act, block, way, False))

    barrier = pltpu.get_barrier_semaphore()
    for way in (up, down, right, left):

        @pl.when(exists[way])
        def _(way=way):
            pl.semaphore_signal(
                barrier, inc=1, device_id={"col": col + step[way]},
                device_id_type=pl.DeviceIdType.MESH,
            )

    pl.semaphore_wait(barrier, sum(there.astype(jnp.int32) for there in exists.values()))

    mine = pltpu.make_async_copy(own_ref, place(col), local_sem)
    mine.start()
    walk(
        lambda block, way: copy(block, way).wait_recv(),
        lambda block, way, own: copy(block, way, own).start(),
    )
    walk(
        lambda block, way: None,
        lambda block, way, own: copy(block, way, own).wait_send(),
    )
    mine.wait()


def gather_columns(block, columns, collective_id):
    nz, nx = CHIPS_Z, columns // CHIPS_Z
    rows, width = block.shape
    return pl.pallas_call(
        functools.partial(gather_kernel, nz, nx),
        out_shape=jax.ShapeDtypeStruct((rows, width * columns), block.dtype),
        in_specs=[pl.BlockSpec(memory_space=pl.ANY)],
        out_specs=pl.BlockSpec(memory_space=pl.ANY),
        scratch_shapes=[
            pltpu.SemaphoreType.DMA((4, columns)),
            pltpu.SemaphoreType.DMA((columns,)),
            pltpu.SemaphoreType.DMA,
        ],
        compiler_params=pltpu.CompilerParams(
            collective_id=collective_id, has_side_effects=True
        ),
        cost_estimate=pl.CostEstimate(
            flops=0, bytes_accessed=300 * rows * width * 4, transcendentals=0
        ),
        name="gather_columns_%d" % collective_id,
    )(block)


def dot(left, right, contract):
    return lax.dot_general(
        left,
        right,
        ((contract, contract) if contract == (0,) else ((1,), (0,)), ((), ())),
        precision=lax.Precision.HIGH,
        preferred_element_type=jnp.float32,
    )


def per_device(n_row, n_col, sigma_top, factor_cross, factor_inverse, block_inverse, ancestors):
    height, width = sigma_top.shape
    living_rows = ancestors.shape[0] * BLK
    chunk = living_rows // n_row
    unit = BLK
    while chunk % unit:
        unit //= 2
    row = lax.axis_index("row")

    def living_chunk(strip):
        parts = []
        for i in range(chunk // unit):
            at = row * chunk + i * unit
            start = ancestors[at // BLK] * BLK + at % BLK
            parts.append(lax.dynamic_slice(strip, (start, 0), (unit, strip.shape[1])))
        return jnp.concatenate(parts, axis=0)

    def over_row(array):
        return lax.all_gather(array, "row", axis=0, tiled=True)

    cross_strip = over_row(factor_cross)
    factor_inverse, cross_strip = lax.optimization_barrier((factor_inverse, cross_strip))
    inverse_strip = over_row(factor_inverse)
    sigma_top, inverse_strip = lax.optimization_barrier((sigma_top, inverse_strip))
    top_strip = over_row(sigma_top)

    cross = gather_columns(living_chunk(cross_strip), n_col, 1)
    update = dot(cross, inverse_strip, (1,))
    update_strip = over_row(update)
    update_wide = gather_columns(update, n_col, 2)

    shares = []
    for shift in range(n_row):
        to = lax.rem(row + shift, n_row)
        piece = lax.dynamic_slice(update_wide, (0, to * height), (chunk, height))
        if shift:
            piece = lax.ppermute(
                piece, "row", [(i, (i + shift) % n_row) for i in range(n_row)]
            )
        shares.append(piece)

    top_chunk, update_wide = lax.optimization_barrier((living_chunk(top_strip), update_wide))
    top = gather_columns(top_chunk, n_col, 3)
    top = jnp.concatenate(
        [
            lax.dynamic_slice(top, (0, ancestors[i] * BLK), (chunk, BLK))
            for i in range(ancestors.shape[0])
        ],
        axis=1,
    )
    living_cross = over_row(-dot(top, update_strip, (1,)))

    blocks = []
    for i in range(height // BLK):
        match = ancestors == row * (height // BLK) + i
        start = jnp.argmax(match).astype(jnp.int32) * BLK
        rows = lax.dynamic_slice(living_cross, (start, 0), (BLK, width))
        blocks.append(jnp.where(jnp.any(match), rows, jnp.float32(0.0)))
    sigma_cross = jnp.concatenate(blocks, axis=0)

    sigma_child = block_inverse
    for shift in range(n_row):
        source = lax.rem(row - shift + n_row, n_row)
        rows = lax.dynamic_slice(living_cross, (source * chunk, 0), (chunk, width))
        sigma_child = sigma_child - dot(shares[shift], rows, (0,))
    return (sigma_cross, sigma_child)


def solution(mesh):
    return jax.shard_map(
        functools.partial(per_device, mesh.shape["row"], mesh.shape["col"]),
        mesh=mesh,
        in_specs=(P("row", "col"), P("row", "col"), P("row", "col"), P("row", "col"), P()),
        out_specs=(P("row", "col"), P("row", "col")),
        check_vma=False,
    )
```

time: 2860 us -> 1250 us (0.44)
  waiting for transfers between devices: 2430 us -> 440 us
  Pallas kernels: 0 us -> 616 us
  matrix products: 401 us -> 89.8 us
  local copies, waits for them, and re-layouts: 6.05 us -> 42.3 us
    all_gather x5, waiting for transfers between devices: 2290 us -> 331 us  [over_row(): return lax.all_gather(array, 'row', axis=0, tiled=True)]
    pallas_call x0 -> x3, Pallas kernels: none -> 616 us  [gather_columns(): pl.pallas_call(functools.partial(gather_kernel, nz, nx), out_shape=jax.Sh...]
    dot_general x3 -> x6, matrix products: 401 us -> 89.8 us  [dot(): lax.dot_general(left, right, ((contract, contract) if contract == (0,) el...]
    reduce_scatter x1 -> x0, waiting for transfers between devices: 134 us -> none  [per_device(): lax.psum_scatter(transposed_rows(gathered, update), 'row', scatter_dimens...]
    ppermute x0 -> x3, waiting for transfers between devices: none -> 108 us  [per_device(): lax.ppermute(piece, 'row', [(i, (i + shift) % n_row) for i in range(n_row)])]
  transfers between devices with their start and end apart: 6 -> 8, of which waited for: 6 -> 5; matrix products, arithmetic and copies ran while one was open for 4% -> 10% of each run, Pallas kernels for 0% -> 50%
where the time goes in v1:
time: 1250 us; the launch traced here: 1240 us
  Pallas kernels  616 us (49%)
  waiting for transfers between devices  440 us (35%)
  matrix products  89.8 us (7%)
  local copies, waits for them, and re-layouts  42.3 us (3%)
  between operations  27.3 us (2%)
  other arithmetic  25 us (2%)
    pallas_call x3, Pallas kernels, gather_columns(): pl.pallas_call(functools.partial(gather_kernel, nz, nx), out_shape=jax.Sh...  616 us
    all_gather x5, waiting for transfers between devices, over_row(): return lax.all_gather(array, 'row', axis=0, tiled=True)  331 us
    ppermute x3, waiting for transfers between devices, per_device(): lax.ppermute(piece, 'row', [(i, (i + shift) % n_row) for i in range(n_row)])  108 us
    dot_general x6, matrix products, dot(): lax.dot_general(left, right, ((contract, contract) if contract == (0,) el...  89.8 us
  transfers between devices with their start and end apart: 8, of which 5 were waited for; matrix products, arithmetic and copies ran while one was open for 10% of the time, Pallas kernels for 50%

profile of v1, /device:TPU:0, one launch (start us, length us, event | category | flops | bytes accessed | tf_op | source)
XLA Modules:
  0.0 1242.4 jit_solution(5981221104920875504)
XLA Ops:
  7.2 0.0 copy-start.1
  7.2 0.0 all-gather.6.cloned.1.call-start
  7.2 0.7 all-gather.6.cloned.1.call-update
  7.9 0.0 all-gather.8.cloned.1.call-start
  8.0 124.4 %all-gather.6.cloned.1.call-done = f32[6144,768]{1,0:T(8,128)} async-done(((f32[1536,768]{1,0:T(8,128)}), f32[6144,768]{1,0:T(8,128)}) %all-gather.6.cloned.1.call-update) | async-done | bytes 18874384 | tf_op jit(solution)/shard_map/all_gather | solution.py:134
  132.3 0.0 all-gather.8.cloned.1.call-update
  132.4 0.0 all-gather.10.cloned.1.call-start
  132.4 121.6 %all-gather.8.cloned.1.call-done = f32[6144,768]{1,0:T(8,128)} async-done(((f32[1536,768]{1,0:T(8,128)}), f32[6144,768]{1,0:T(8,128)}) %all-gather.8.cloned.1.call-update) | async-done | bytes 18874384 | tf_op jit(solution)/shard_map/all_gather | solution.py:134
  254.0 0.0 all-gather.10.cloned.1.call-update
  254.0 0.0 all-gather.12.cloned.1.call-start
  254.1 0.0 copy-done.1
  254.1 0.7 fusion.15
  256.7 1.8 constant_dynamic-slice_fusion.5
  258.5 1.6 pad_maximum_fusion.1.own_ref
  260.1 210.4 %gather_columns_1.1 = f32[768,6144]{1,0:T(8,128)} custom-call(f32[768,768]{1,0:T(8,128)} %pad_maximum_fusion.1.own_ref), custom_call_target="tpu_custom_call" | custom-call | bytes 707788800 | tf_op jit(solution)/shard_map/gather_columns_1/pallas_call | solution.py:86
  470.5 28.8 %fusion.16.own_ref = f32[768,768]{1,0:T(8,128)} fusion(f32[768,6144]{1,0:T(8,128)} %gather_columns_1.1, f32[6144,768]{1,0:T(8,128)} %all-gather.8.cloned.1.call-done), kind=kOutput, calls=%fused_computation.57 | convolution fusion | flops 21743271936 | bytes 40108032 | tf_op jit(solution)/shard_map/dot_general | solution.py:107
  499.3 0.0 all-gather.12.cloned.1.call-update
  499.3 0.0 all-gather.14.cloned.1.call-start
  506.6 203.3 %gather_columns_2.1 = f32[768,6144]{1,0:T(8,128)} custom-call(f32[768,768]{1,0:T(8,128)} %fusion.16.own_ref), custom_call_target="tpu_custom_call" | custom-call | bytes 707788800 | tf_op jit(solution)/shard_map/gather_columns_2/pallas_call | solution.py:86
  709.8 0.0 all-gather.10.cloned.1.call-done
  709.9 1.8 constant_dynamic-slice_fusion.8
  711.7 1.6 pad_maximum_fusion.own_ref
  713.3 202.6 %gather_columns_3.1 = f32[768,6144]{1,0:T(8,128)} custom-call(f32[768,768]{1,0:T(8,128)} %pad_maximum_fusion.own_ref), custom_call_target="tpu_custom_call" | custom-call | bytes 707788800 | tf_op jit(solution)/shard_map/gather_columns_3/pallas_call | solution.py:86
  915.9 2.1 dynamic-slice_dynamic-update-slice_fusion.11
  918.0 2.1 dynamic-slice_dynamic-update-slice_fusion.10
  920.1 2.1 dynamic-slice_dynamic-update-slice_fusion.9
  922.2 2.1 dynamic-slice_dynamic-update-slice_fusion.8
  924.3 2.1 dynamic-slice_dynamic-update-slice_fusion.7
  926.4 2.1 dynamic-slice_dynamic-update-slice_fusion.6
  928.5 2.1 dynamic-slice_dynamic-update-slice_fusion.5
  930.6 2.1 dynamic-slice_dynamic-update-slice_fusion.4
  932.7 2.1 dynamic-slice_dynamic-update-slice_fusion.3
  934.8 2.1 dynamic-slice_dynamic-update-slice_fusion.2
  936.9 2.1 dynamic-slice_dynamic-update-slice_fusion.1
  939.0 2.1 dynamic-slice_dynamic-update-slice_fusion
  941.1 0.0 all-gather.12.cloned.1.call-done
  941.1 16.4 %convolution_negate_fusion = f32[768,768]{1,0:T(8,128)} fusion(f32[768,3072]{1,0:T(8,128)} %dynamic-slice_dynamic-update-slice_fusion, f32[3072,768]{1,0:T(8,128)} %all-gather.12.cloned.1.call-done), kind=kOutput, calls=%fused_computation.12 | convolution fusion | flops 10872225792 | bytes 21233664 | tf_op jit(solution)/shard_map/dot_general | solution.py:107
  957.5 0.0 all-gather.14.cloned.1.call-update
  957.6 12.6 %constant_dynamic-slice_fusion = (f32[768,1536]{1,0:T(8,128)}, f32[768,1536]{1,0:T(8,128)}, f32[768,1536]{1,0:T(8,128)}) fusion(f32[768,6144]{1,0:T(8,128)} %gather_columns_2.1, s32[]{:T(128)S(6)} %select_n.236, s32[]{:T(128)S(6)} %select_n.234, s32[]{:T(128)S(6)} %select_n.232), kind=kLoop, calls=%fused_computation.31 | loop fusion | bytes 28311564 | tf_op jit(solution)/shard_map/dynamic_slice | solution.py:150
  970.2 0.0 collective-permute-start
  970.2 0.3 collective-permute-start.1
  970.5 1.5 collective-permute-start.2
  972.0 0.7 compare_reduce_fusion.10
  973.4 0.7 compare_reduce_fusion.8
  974.8 0.7 compare_reduce_fusion.6
  976.3 0.7 compare_reduce_fusion.4
  977.7 0.7 compare_reduce_fusion.2
  979.1 0.7 compare_reduce_fusion
  980.6 0.7 compare_reduce_fusion.1
  981.4 85.1 %all-gather.14.cloned.1.call-done = f32[3072,768]{1,0:T(8,128)} async-done(((f32[768,768]{1,0:T(8,128)}), f32[3072,768]{1,0:T(8,128)}) %all-gather.14.cloned.1.call-update) | async-done | bytes 9437200 | tf_op jit(solution)/shard_map/all_gather | solution.py:134
  1066.5 3.0 select_dynamic-update-slice_fusion.5
  1069.4 2.9 select_dynamic-update-slice_fusion.4
  1072.4 2.7 select_dynamic-update-slice_fusion.3
  1075.1 2.8 select_dynamic-update-slice_fusion.2
  1077.9 2.6 select_dynamic-update-slice_fusion.1
  1080.5 2.7 select_dynamic-update-slice_fusion
  1083.2 0.0 copy-done
  1083.2 9.9 fusion
  1093.1 26.9 %collective-permute-done = f32[768,1536]{1,0:T(8,128)} collective-permute-done((f32[768,1536]{1,0:T(8,128)}, f32[768,1536]{1,0:T(8,128)}, u32[]{:S(2)}, u32[]{:S(2)}) %collective-permute-start) | collective-permute-done | bytes 4718624 | tf_op jit(solution)/shard_map/ppermute | solution.py:152
  1120.0 9.0 fusion.8
  1129.0 0.0 collective-permute-done.1
  1129.0 9.0 fusion.6
  1138.1 81.1 %collective-permute-done.2 = f32[768,1536]{1,0:T(8,128)} collective-permute-done((f32[768,1536]{1,0:T(8,128)}, f32[768,1536]{1,0:T(8,128)}, u32[]{:S(2)}, u32[]{:S(2)}) %collective-permute-start.2) | collective-permute-done | bytes 4718624 | tf_op jit(solution)/shard_map/ppermute | solution.py:152
  1219.2 16.7 %subtract_subtract_fusion = f32[1536,768]{1,0:T(8,128)} fusion(f32[1536,768]{1,0:T(8,128)S(1)} %fusion.6, f32[1536,768]{1,0:T(8,128)S(1)} %fusion.8, f32[1536,768]{1,0:T(8,128)} %param.8, f32[1536,768]{1,0:T(8,128)} %fusion, f32[768,1536]{1,0:T(8,128)} %collective-permute-done.2, f32[3072,768]{1,0:T(8,128)S(1)} %copy-done, s32[]{:T(128)S(6)} %select_n.237), kind=kOutput, calls=%fused_computation | convolution fusion | flops 5440536576 | bytes 30670852 | tf_op jit(solution)/shard_map/dot_general | solution.py:107
  (1 shorter events, 0.0 us)
Async XLA Ops:
  7.2 246.9 %copy-start.1 = (s32[12]{0:T(128)S(1)}, s32[12]{0:T(128)}, u32[]{:S(2)}) copy-start(s32[12]{0:T(128)} %param.9) | copy-start | bytes 148
  7.2 125.2 %all-gather.6.cloned.1.call-start = ((), (), s32[]{:S(2)}) async-start(), calls=%async_computation | async-start | bytes 23592960 | tf_op jit(solution)/shard_map/all_gather | solution.py:134
  7.9 246.0 %all-gather.8.cloned.1.call-start = ((), (), s32[]{:S(2)}) async-start(), calls=%async_computation.1 | async-start | bytes 23592960 | tf_op jit(solution)/shard_map/all_gather | solution.py:134
  132.4 577.5 %all-gather.10.cloned.1.call-start = ((), (), s32[]{:S(2)}) async-start(), calls=%async_computation.2 | async-start | bytes 23592960 | tf_op jit(solution)/shard_map/all_gather | solution.py:134
  254.0 687.2 %all-gather.12.cloned.1.call-start = ((), (), s32[]{:S(2)}) async-start(), calls=%async_computation.3 | async-start | bytes 11796480 | tf_op jit(solution)/shard_map/all_gather | solution.py:134
  499.3 567.2 %all-gather.14.cloned.1.call-start = ((), (), s32[]{:S(2)}) async-start(), calls=%async_computation.4 | async-start | bytes 11796480 | tf_op jit(solution)/shard_map/all_gather | solution.py:134
  970.2 149.8 %collective-permute-start = (f32[768,1536]{1,0:T(8,128)}, f32[768,1536]{1,0:T(8,128)}, u32[]{:S(2)}, u32[]{:S(2)}) collective-permute-start(f32[768,1536]{1,0:T(8,128)} %get-tuple-element.32), channel_id=1, source_target_pairs={{0,8},{8,16},{16,24},{24,0},{1,9},{9,17},{17,25},{25,1},{2,10},{10... | collective-permute-start | bytes 14155784 | tf_op jit(solution)/shard_map/ppermute | solution.py:152
  970.2 158.9 %collective-permute-start.1 = (f32[768,1536]{1,0:T(8,128)}, f32[768,1536]{1,0:T(8,128)}, u32[]{:S(2)}, u32[]{:S(2)}) collective-permute-start(f32[768,1536]{1,0:T(8,128)} %get-tuple-element.31), channel_id=1, source_target_pairs={{0,16},{8,24},{16,0},{24,8},{1,17},{9,25},{17,1},{25,9},{2,18},{10... | collective-permute-start | bytes 14155784 | tf_op jit(solution)/shard_map/ppermute | solution.py:152
  970.5 248.7 %collective-permute-start.2 = (f32[768,1536]{1,0:T(8,128)}, f32[768,1536]{1,0:T(8,128)}, u32[]{:S(2)}, u32[]{:S(2)}) collective-permute-start(f32[768,1536]{1,0:T(8,128)} %get-tuple-element.30), channel_id=1, source_target_pairs={{0,24},{8,0},{16,8},{24,16},{1,25},{9,1},{17,9},{25,17},{2,26},{10... | collective-permute-start | bytes 14155784 | tf_op jit(solution)/shard_map/ppermute | solution.py:152
  1066.5 16.7 %copy-start = (f32[3072,768]{1,0:T(8,128)S(1)}, f32[3072,768]{1,0:T(8,128)}, u32[]{:S(2)}) copy-start(f32[3072,768]{1,0:T(8,128)} %all-gather.14.cloned.1.call-done) | copy-start | bytes 28311556
Sparse Core Ops, SparseCore 0:
  9.6 122.7 all-gather.5
  133.9 120.0 all-gather.7
  255.5 120.0 all-gather.9
  499.4 61.4 all-gather.11
  957.7 108.7 all-gather.13
